TPU v7x, 512 devices: a whole 4x8x8 slice. The times are simulated.
512 devices in a mesh: section: 32 (over z, x_hi, core), tensor: 16 (over x_lo, y).
Axes of the slice: x: 4 (x_hi: 2, x_lo: 2; x = x_hi * 2 + x_lo), y: 8, z: 8, core: 2. Of those that a mesh axis runs over, the one named last changes fastest.
Arguments:
- held: bfloat16 [32, 2, 256, 12288], P('section', None, None, 'tensor'), may hold values from -6 to 6
- norm_gain: float32 [32, 2, 12288], P('section', None, 'tensor'), may hold values from 0.1 to 1.9
- key_gain: float32 [32, 2, 12288], P('section', None, 'tensor'), may hold values from -2 to 2
- evict_slot: int32 [32], P('section'), may hold values from 0 to 1
- evict_step: int32 [32], P('section'), may hold values from 0 to 1
Outputs:
- final: bfloat16 [32, 2, 256, 12288], P('section', None, None, 'tensor')
- mirror_store: bfloat16 [32, 256, 12288], P('section', None, 'tensor')
All inputs are finite; a program needn't handle non-finite values.
Results may differ from a plain program's by a relative error of at most 0.039.
Values may be sent and summed in bfloat16 or wider, within the bound.
No kernel may reach another device: no remote copies, remote signals or barrier semaphores. Data moves between devices by JAX's collectives and lax.ppermute only.
A program may use at most 64 MiB of HBM per device.

v0:
```python
import functools

import jax
import jax.numpy as jnp
from jax import lax
from jax.experimental import pallas as pl
from jax.experimental.pallas import tpu as pltpu
from jax.sharding import PartitionSpec as P

D = 12288
HEAD = 128
LAYERS = 2
BLOCK = 128
EPS = 1e-5
SCORE = 1.4426950408889634 / HEAD**0.5
X_LO = X_HI = CORES = 2

VMEM = pl.BlockSpec(memory_space=pltpu.VMEM)
PARAMS = pltpu.CompilerParams(vmem_limit_bytes=32 * 1024 * 1024)


def call(kernel, out_shape, name, mflop=1):
    several = isinstance(out_shape, tuple)

    def run(*operands):
        return pl.pallas_call(
            kernel,
            out_shape=out_shape,
            in_specs=[VMEM] * len(operands),
            out_specs=(VMEM,) * len(out_shape) if several else VMEM,
            compiler_params=PARAMS,
            cost_estimate=pl.CostEstimate(
                flops=mflop * 1_000_000, bytes_accessed=1_000_000, transcendentals=mflop * 2_000
            ),
            name=name,
        )(*operands)

    return run


def f32(*shape):
    return jax.ShapeDtypeStruct(shape, jnp.float32)


def bf16(*shape):
    return jax.ShapeDtypeStruct(shape, jnp.bfloat16)


def column(total):
    inv = lax.rsqrt(total / D + EPS)
    rows = [jnp.broadcast_to(inv[i : i + 1], (BLOCK, BLOCK)).T for i in range(inv.shape[0])]
    return jnp.concatenate(rows, axis=0)


def head_layer(xf, scale, ngain, kgain):
    length = xf.shape[0]
    keep = lax.broadcasted_iota(jnp.int32, (BLOCK, BLOCK), 1) <= lax.broadcasted_iota(jnp.int32, (BLOCK, BLOCK), 0)
    h = xf * scale * ngain
    query = h.astype(jnp.bfloat16)
    keys = (h * (kgain * SCORE)).astype(jnp.bfloat16)
    values = jnp.concatenate([query, jnp.ones((length, HEAD), jnp.bfloat16)], axis=1)
    out = []
    for i in range(length // BLOCK):
        here = slice(i * BLOCK, (i + 1) * BLOCK)
        seen = (i + 1) * BLOCK
        s = lax.dot_general(
            query[here], keys[:seen], (((1,), (1,)), ((), ())), preferred_element_type=jnp.float32
        )
        last = jnp.where(keep, s[:, i * BLOCK :], jnp.float32(-1e30))
        s = last if i == 0 else jnp.concatenate([s[:, : i * BLOCK], last], axis=1)
        p = jnp.exp2(s - jnp.max(s, axis=1, keepdims=True)).astype(jnp.bfloat16)
        o = jnp.dot(p, values[:seen], preferred_element_type=jnp.float32)
        out.append((xf[here] + o[:, :HEAD] / o[:, HEAD:]).astype(jnp.bfloat16))
    return jnp.concatenate(out, axis=0)


def token_sums(squares, out_ref):
    rows = []
    for sq in squares:
        for i in range(sq.shape[0] // BLOCK):
            rows.append(jnp.sum(sq[i * BLOCK : (i + 1) * BLOCK].T, axis=0, keepdims=True))
    out_ref[...] = jnp.broadcast_to(jnp.concatenate(rows, axis=0)[None], out_ref.shape)


def lanes(head):
    return slice(head * HEAD, (head + 1) * HEAD)


class Pack:
    def __init__(self, heads, batch, blocks):
        self.heads, self.rows = heads, batch * blocks
        self.sums = slice(2 * LAYERS * heads, 2 * LAYERS * heads + self.rows)
        self.slot = self.sums.stop
        self.step = self.slot + 1
        self.size = -(-(self.step + 1) // 8) * 8

    def gains(self, ref, layer, head):
        at = [(part * LAYERS + layer) * self.heads + head for part in range(2)]
        return [ref[i : i + 1, :] for i in at]

    def second(self, ref):
        return ref[self.slot : self.slot + 1, :] > 0.5

    def late(self, ref):
        return ref[self.step : self.step + 1, :] > 0.5


def first_kernel(x_ref, out_ref):
    batch, _, width = x_ref.shape
    found = []
    for b in range(batch):
        sq = 0.0
        for head in range(width // HEAD):
            xf = x_ref[b, :, lanes(head)].astype(jnp.float32)
            sq = sq + xf * xf
        found.append(sq)
    token_sums(found, out_ref)


def layer_kernel(pack, layer, split, outputs, *refs):
    x_refs = refs[:2] if split else [refs[0].at[b] for b in range(refs[0].shape[0])]
    refs = list(refs[2 if split else 1 :])
    parts_ref = refs.pop(0) if "parts" in outputs else None
    pack_ref = refs.pop(0)
    y_ref = refs.pop(0) if "y" in outputs else None
    pick_ref = refs.pop(0) if "pick" in outputs else None
    sums_ref = refs.pop(0) if "sums" in outputs else None
    blocks = x_refs[0].shape[0] // BLOCK
    totals = pack_ref[pack.sums, :] if parts_ref is None else jnp.sum(parts_ref[...], axis=0)
    found = []
    for b, x_ref in enumerate(x_refs):
        scale = column(totals[b * blocks : (b + 1) * blocks])
        sq = 0.0
        for head in range(pack.heads):
            xf = x_ref[:, lanes(head)].astype(jnp.float32)
            y = head_layer(xf, scale, *pack.gains(pack_ref, layer, head))
            if y_ref is not None:
                y_ref[b, :, lanes(head)] = y
            if sums_ref is not None:
                yf = y.astype(jnp.float32)
                sq = sq + yf * yf
        found.append(sq)
    if pick_ref is not None:
        second = pack.second(pack_ref)
        for head in range(pack.heads):
            pick_ref[:, lanes(head)] = either(second, y_ref[1, :, lanes(head)], y_ref[0, :, lanes(head)])
    if sums_ref is not None:
        token_sums(found, sums_ref)


def either(condition, there, here):
    return jnp.where(condition, there.astype(jnp.float32), here.astype(jnp.float32)).astype(jnp.bfloat16)


def pack_kernel(pack, parts_ref, rest_ref, out_ref):
    out_ref[...] = rest_ref[...]
    out_ref[pack.sums, :] = jnp.sum(parts_ref[...], axis=0)


def choose_kernel(pack, y_ref, carry_ref, pack_ref, out_ref):
    second, late = pack.second(pack_ref), pack.late(pack_ref)
    for head in range(pack.heads):
        at = lanes(head)
        out_ref[:, at] = either(late, either(second, y_ref[1, :, at], y_ref[0, :, at]), carry_ref[:, at])


def mirror_kernel(pack, layer, x_ref, *refs):
    *parts_ref, pack_ref, out_ref = refs
    kept_ref = parts_ref.pop(0) if layer else x_ref
    blocks = x_ref.shape[0] // BLOCK
    totals = jnp.sum(parts_ref[0][...], axis=0) if parts_ref else pack_ref[pack.sums, :]
    scale = column(jnp.where(pack.second(pack_ref), totals[blocks : 2 * blocks], totals[:blocks]))
    late = pack.late(pack_ref)
    for head in range(pack.heads):
        xf = x_ref[:, lanes(head)].astype(jnp.float32)
        y = head_layer(xf, scale, *pack.gains(pack_ref, layer, head))
        out_ref[:, lanes(head)] = either(late, y, kept_ref[:, lanes(head)])


def exchange(parts):
    return lax.all_to_all(parts, "tensor", 0, 0, tiled=True)


def send(value, target):
    count = lax.axis_size("section")
    return lax.ppermute(value, "section", [(s, target(s) % count) for s in range(count)])


def around_x(hop):
    sections, members = lax.axis_size("section"), lax.axis_size("tensor")
    ys, count = members // X_LO, X_HI * X_LO
    layers_z = sections // (X_HI * CORES)

    def flat(z, x, core, y):
        x %= count
        return (((z % layers_z) * X_HI + x // X_LO) * CORES + core) * members + (x % X_LO) * ys + y

    pairs = []
    for z in range(layers_z):
        for x in range(count):
            for core in range(CORES):
                for y in range(ys):
                    middle = flat(z, x - 1, core, y)
                    pairs.append(
                        (middle, flat(z + x // X_LO, x - 2, core, y)) if hop else (flat(z, x, core, y), middle)
                    )
    return pairs


def after(value, *earlier):
    return lax.optimization_barrier((value, *earlier))[0]


def shards(held, norm_gain, key_gain, evict_slot, evict_step):
    x = held[0]
    batch, length, width = x.shape
    heads = width // HEAD
    pack = Pack(heads, batch, length // BLOCK)
    sections, members = lax.axis_size("section"), lax.axis_size("tensor")
    both, one = bf16(*x.shape), bf16(length, width)
    sums = f32(members, pack.rows, BLOCK)
    axes = ("section", "tensor")

    def layer(at, outputs, split=False):
        shapes = {"y": both, "pick": one, "sums": sums}
        out = tuple(shapes[name] for name in ("y", "pick", "sums") if name in outputs)
        return call(functools.partial(layer_kernel, pack, at, split, outputs), out, "_".join(outputs), 400)

    facts = jnp.concatenate([evict_slot, evict_step]).astype(jnp.float32)
    head = jnp.concatenate(
        [
            norm_gain.reshape(-1, HEAD),
            key_gain.reshape(-1, HEAD),
            jnp.zeros((pack.rows, HEAD), jnp.float32),
            jnp.broadcast_to(facts[:, None], (2, HEAD)),
            jnp.zeros((pack.size - pack.step - 1, HEAD), jnp.float32),
        ],
        axis=0,
    )

    found = call(first_kernel, sums, "first_sums")(x)
    second_half = lax.ppermute(after(x[1], found), axes, around_x(0))
    first_ahead = send(after(x[0], found), lambda s: s + 2)
    parts = exchange(found)
    own = call(functools.partial(pack_kernel, pack), f32(pack.size, HEAD), "own_pack")(parts, head)
    (found,) = layer(0, ("parts", "sums"))(x, parts, head)
    second_ahead = lax.ppermute(after(second_half, found), axes, around_x(1))
    behind2 = send(after(own, found), lambda s: s + 2)
    behind = send(after(own, found), lambda s: s + 1)
    parts = send(exchange(found), lambda s: s + 2)

    (y,) = layer(0, ("y",), split=True)(after(first_ahead, behind), second_ahead, behind2)
    y, pick, found = layer(1, ("parts", "y", "pick", "sums"))(y, parts, behind2)
    carry = send(after(pick, found), lambda s: s - 1)
    parts = exchange(found)
    chosen = call(functools.partial(choose_kernel, pack), one, "choose")(y, after(carry, parts), behind)
    kept = send(chosen, lambda s: -s)
    late = call(functools.partial(pack_kernel, pack), f32(pack.size, HEAD), "late_pack")(parts, behind)
    y, found = layer(0, ("parts", "y", "sums"))(y, parts, behind)
    late = send(after(late, found), lambda s: -s)
    parts = exchange(found)
    there = send(parts, lambda s: -s)
    (final,) = layer(1, ("parts", "y"))(y, parts, behind)

    stored = call(functools.partial(mirror_kernel, pack, 0), one, "mirror_third", 200)(kept, late)
    stored = call(functools.partial(mirror_kernel, pack, 1), one, "mirror_fourth", 200)(stored, kept, there, late)
    return (final[None], stored[None])


def solution(mesh):
    return jax.shard_map(
        shards,
        mesh=mesh,
        in_specs=(
            P("section", None, None, "tensor"),
            P("section", None, "tensor"),
            P("section", None, "tensor"),
            P("section"),
            P("section"),
        ),
        out_specs=(P("section", None, None, "tensor"), P("section", None, "tensor")),
        check_vma=False,
    )
```

profile of v0, /device:TPU:128, one launch (start us, length us, event | category | flops | bytes accessed | tf_op | source)
XLA Modules:
  0.0 105.4 jit_solution(2809505988308582616)
XLA Ops:
  0.6 0.0 copy-start
  0.6 1.2 %slice_bitcast_fusion = (bf16[256,768]{1,0:T(8,128)(2,1)S(1)}, bf16[256,768]{1,0:T(8,128)(2,1)S(1)}) fusion(bf16[1,2,256,768]{3,2,1,0:T(8,128)(2,1)} %param.5), kind=kLoop, calls=%fused_computation | loop fusion | bytes 1572864 | tf_op jit(solution)/shard_map/squeeze | solution.py:242
  1.9 0.1 copy-done
  2.0 0.8 first_sums.1
  2.8 4.7 %collective-permute-start.2 = (bf16[256,768]{1,0:T(8,128)(2,1)S(1)}, bf16[256,768]{1,0:T(8,128)(2,1)S(1)}, u32[]{:S(2)}, u32[]{:S(2)}) collective-permute-start(bf16[256,768]{1,0:T(8,128)(2,1)S(1)} %get-tuple-element.18), channel_id=1, source_target_pairs={{0,40},{1,41},{2,42},{3,43},{4,44},{5,45},{6,46},{7,47},{16,56},{1... | collective-permute-start | bytes 1179656 | tf_op jit(solution)/shard_map/ppermute | solution.py:242
  7.5 0.0 copy-start.1
  7.5 7.2 %all-to-all-start = ((f32[16,4,128]{2,1,0:T(4,128)}), f32[16,4,128]{2,1,0:T(4,128)S(1)}, u32[]{:S(2)}, u32[]{:S(2)}) async-start(f32[16,4,128]{2,1,0:T(4,128)} %first_sums.1), calls=%async_computation | async-start | bytes 65536 | tf_op jit(solution)/shard_map/all_to_all | solution.py:181
  14.7 3.6 %collective-permute-start = (bf16[256,768]{1,0:T(8,128)(2,1)S(1)}, bf16[256,768]{1,0:T(8,128)(2,1)S(1)}, u32[]{:S(2)}, u32[]{:S(2)}) collective-permute-start(bf16[256,768]{1,0:T(8,128)(2,1)S(1)} %get-tuple-element.15), channel_id=1, source_target_pairs={{0,32},{16,48},{32,64},{48,80},{64,96},{80,112},{96,128},{112,144}... | collective-permute-start | bytes 1179656 | tf_op jit(solution)/shard_map/ppermute | solution.py:186
  19.7 0.0 copy-done.1
  19.7 0.0 copy-start.2
  19.7 0.7 copy-done.2
  20.4 0.1 add_convert_fusion
  20.5 0.1 broadcast_in_dim.19
  20.5 0.1 concatenate.11.rest_ref.refs_2_
  20.7 2.7 %all-to-all-done.parts_ref.refs_1_ = f32[16,4,128]{2,1,0:T(4,128)S(1)} async-done(((f32[16,4,128]{2,1,0:T(4,128)}), f32[16,4,128]{2,1,0:T(4,128)S(1)}, u32[]{:S(2)}, u32[]{:S(2)}) %all-to-all-start) | async-done | bytes 32800 | tf_op jit(solution)/shard_map/all_to_all | solution.py:181
  23.3 2.4 %parts_sums.1 = f32[16,4,128]{2,1,0:T(4,128)} custom-call(bf16[2,256,768]{2,1,0:T(8,128)(2,1)S(1)} %bitcast.8, f32[16,4,128]{2,1,0:T(4,128)S(1)} %all-to-all-done.parts_ref.refs_1_, f32[32,128]{1,0:T(8,128)S(1)} %concatenate.11.rest_ref.refs_2_), custom_call_target="tpu_custom_call" | custom-call | flops 400000000 | bytes 1000000 | tf_op jit(solution)/shard_map/parts_sums/pallas_call | solution.py:26
  25.8 0.0 collective-permute-done.2
  25.8 3.9 %collective-permute-start.3 = (bf16[256,768]{1,0:T(8,128)(2,1)S(1)}, bf16[256,768]{1,0:T(8,128)(2,1)S(1)}, u32[]{:S(2)}, u32[]{:S(2)}) collective-permute-start(bf16[256,768]{1,0:T(8,128)(2,1)S(1)} %collective-permute-done.2), channel_id=1, source_target_pairs={{40,32},{41,33},{42,34},{43,35},{44,36},{45,37},{46,38},{47,39},{5... | collective-permute-start | bytes 1179656 | tf_op jit(solution)/shard_map/ppermute | solution.py:247
  29.7 6.8 %all-to-all-start.1 = ((f32[16,4,128]{2,1,0:T(4,128)}), f32[16,4,128]{2,1,0:T(4,128)S(1)}, u32[]{:S(2)}, u32[]{:S(2)}) async-start(f32[16,4,128]{2,1,0:T(4,128)} %parts_sums.1), calls=%async_computation.1 | async-start | bytes 65536 | tf_op jit(solution)/shard_map/all_to_all | solution.py:181
  36.5 1.9 %collective-permute-start.1 = (f32[32,128]{1,0:T(8,128)S(1)}, f32[32,128]{1,0:T(8,128)S(1)}, u32[]{:S(2)}, u32[]{:S(2)}) collective-permute-start(f32[32,128]{1,0:T(8,128)S(1)} %own_pack.1), channel_id=1, source_target_pairs={{0,16},{16,32},{32,48},{48,64},{64,80},{80,96},{96,112},{112,128},... | collective-permute-start | bytes 49160 | tf_op jit(solution)/shard_map/ppermute | solution.py:186
  38.4 2.8 %collective-permute-start.4 = (f32[32,128]{1,0:T(8,128)S(1)}, f32[32,128]{1,0:T(8,128)S(1)}, u32[]{:S(2)}, u32[]{:S(2)}) collective-permute-start(f32[32,128]{1,0:T(8,128)S(1)} %own_pack.1), channel_id=1, source_target_pairs={{0,32},{16,48},{32,64},{48,80},{64,96},{80,112},{96,128},{112,144}... | collective-permute-start | bytes 49160 | tf_op jit(solution)/shard_map/ppermute | solution.py:186
  41.2 3.7 %all-to-all-done.1 = f32[16,4,128]{2,1,0:T(4,128)S(1)} async-done(((f32[16,4,128]{2,1,0:T(4,128)}), f32[16,4,128]{2,1,0:T(4,128)S(1)}, u32[]{:S(2)}, u32[]{:S(2)}) %all-to-all-start.1) | async-done | bytes 32800 | tf_op jit(solution)/shard_map/all_to_all | solution.py:181
  44.9 3.8 %collective-permute-start.5 = (f32[16,4,128]{2,1,0:T(4,128)S(1)}, f32[16,4,128]{2,1,0:T(4,128)S(1)}, u32[]{:S(2)}, u32[]{:S(2)}) collective-permute-start(f32[16,4,128]{2,1,0:T(4,128)S(1)} %all-to-all-done.1), channel_id=1, source_target_pairs={{0,32},{16,48},{32,64},{48,80},{64,96},{80,112},{96,128},{112,144}... | collective-permute-start | bytes 98312 | tf_op jit(solution)/shard_map/ppermute | solution.py:186
  48.8 0.0 collective-permute-done.1.refs_2_.pack_ref.rest_ref
  48.8 0.0 collective-permute-done.refs_0_
  48.8 0.0 collective-permute-done.4.refs_2_
  48.8 0.0 collective-permute-done.3.refs_1_
  48.8 1.7 %y.1.refs_0_ = bf16[2,256,768]{2,1,0:T(8,128)(2,1)S(1)} custom-call(bf16[256,768]{1,0:T(8,128)(2,1)S(1)} %collective-permute-done.refs_0_, bf16[256,768]{1,0:T(8,128)(2,1)S(1)} %collective-permute-done.3.refs_1_, f32[32,128]{1,0:T(8,128)S(1)} %collective-permute-done.4.refs_2_), custom_call_target="tpu_custom_call" | custom-call | flops 400000000 | bytes 1000000 | tf_op jit(solution)/shard_map/y/pallas_call | solution.py:26
  50.5 2.6 %collective-permute-done.5.refs_1_ = f32[16,4,128]{2,1,0:T(4,128)S(1)} collective-permute-done((f32[16,4,128]{2,1,0:T(4,128)S(1)}, f32[16,4,128]{2,1,0:T(4,128)S(1)}, u32[]{:S(2)}, u32[]{:S(2)}) %collective-permute-start.5) | collective-permute-done | bytes 32800 | tf_op jit(solution)/shard_map/ppermute | solution.py:186
  53.1 2.0 %parts_y_pick_sums.1 = (bf16[2,256,768]{2,1,0:T(8,128)(2,1)S(1)}, bf16[256,768]{1,0:T(8,128)(2,1)S(1)}, f32[16,4,128]{2,1,0:T(4,128)S(1)}) custom-call(bf16[2,256,768]{2,1,0:T(8,128)(2,1)S(1)} %y.1.refs_0_, f32[16,4,128]{2,1,0:T(4,128)S(1)} %collective-permute-done.5.refs_1_, f32[32,128]{1,0:T(8,128)S(1)} %collective-permute-done.4.refs_2_), custom_call_target="tpu_custom_call" | custom-call | flops 400000000 | bytes 1000000 | tf_op jit(solution)/shard_map/parts_y_pick_sums/pallas_call | solution.py:26
  55.1 2.8 %collective-permute-start.6 = (bf16[256,768]{1,0:T(8,128)(2,1)S(1)}, bf16[256,768]{1,0:T(8,128)(2,1)S(1)}, u32[]{:S(2)}, u32[]{:S(2)}) collective-permute-start(bf16[256,768]{1,0:T(8,128)(2,1)S(1)} %get-tuple-element.25), channel_id=1, source_target_pairs={{0,496},{16,0},{32,16},{48,32},{64,48},{80,64},{96,80},{112,96},{1... | collective-permute-start | bytes 1179656 | tf_op jit(solution)/shard_map/ppermute | solution.py:186
  58.0 16.4 %all_to_all.20.refs_1_.parts_ref = f32[16,4,128]{2,1,0:T(4,128)S(1)} all-to-all(f32[16,4,128]{2,1,0:T(4,128)S(1)} %get-tuple-element.21), channel_id=1, replica_groups=mesh['section'=32,'tensor'=16] {'tensor'}, dimensions={0} | all-to-all | bytes 65536 | tf_op jit(solution)/shard_map/all_to_all | solution.py:181
  74.4 0.0 collective-permute-done.6.carry_ref
  74.4 0.2 choose.1
  74.5 4.9 %collective-permute-start.7 = (bf16[256,768]{1,0:T(8,128)(2,1)S(1)}, bf16[256,768]{1,0:T(8,128)(2,1)S(1)}, u32[]{:S(2)}, u32[]{:S(2)}) collective-permute-start(bf16[256,768]{1,0:T(8,128)(2,1)S(1)} %choose.1), channel_id=1, source_target_pairs={{0,0},{16,496},{32,480},{48,464},{64,448},{80,432},{96,416},{112,4... | collective-permute-start | bytes 1179656 | tf_op jit(solution)/shard_map/ppermute | solution.py:186
  79.5 2.4 %parts_y_sums.1 = (bf16[2,256,768]{2,1,0:T(8,128)(2,1)S(1)}, f32[16,4,128]{2,1,0:T(4,128)}) custom-call(bf16[2,256,768]{2,1,0:T(8,128)(2,1)S(1)} %get-tuple-element.20.refs_0_.y_ref, f32[16,4,128]{2,1,0:T(4,128)S(1)} %all_to_all.20.refs_1_.parts_ref, f32[32,128]{1,0:T(8,128)S(1)} %collective-permute-done.1.refs_2_.pack_ref.rest_ref), custom_call_target="tpu_custom_call" | custom-call | flops 400000000 | bytes 1000000 | tf_op jit(solution)/shard_map/parts_y_sums/pallas_call | solution.py:26
  81.9 3.5 %all-to-all-start.3 = ((f32[16,4,128]{2,1,0:T(4,128)}), f32[16,4,128]{2,1,0:T(4,128)S(1)}, u32[]{:S(2)}, u32[]{:S(2)}) async-start(f32[16,4,128]{2,1,0:T(4,128)} %get-tuple-element.23), calls=%async_computation.3 | async-start | bytes 65536 | tf_op jit(solution)/shard_map/all_to_all | solution.py:181
  85.4 4.9 %collective-permute-start.8 = (f32[32,128]{1,0:T(8,128)S(1)}, f32[32,128]{1,0:T(8,128)S(1)}, u32[]{:S(2)}, u32[]{:S(2)}) collective-permute-start(f32[32,128]{1,0:T(8,128)S(1)} %late_pack.1), channel_id=1, source_target_pairs={{0,0},{16,496},{32,480},{48,464},{64,448},{80,432},{96,416},{112,4... | collective-permute-start | bytes 49160 | tf_op jit(solution)/shard_map/ppermute | solution.py:186
  90.3 3.6 %all-to-all-done.3.refs_1_ = f32[16,4,128]{2,1,0:T(4,128)S(1)} async-done(((f32[16,4,128]{2,1,0:T(4,128)}), f32[16,4,128]{2,1,0:T(4,128)S(1)}, u32[]{:S(2)}, u32[]{:S(2)}) %all-to-all-start.3) | async-done | bytes 32800 | tf_op jit(solution)/shard_map/all_to_all | solution.py:181
  93.8 4.8 %collective-permute-start.9 = (f32[16,4,128]{2,1,0:T(4,128)S(1)}, f32[16,4,128]{2,1,0:T(4,128)S(1)}, u32[]{:S(2)}, u32[]{:S(2)}) collective-permute-start(f32[16,4,128]{2,1,0:T(4,128)S(1)} %all-to-all-done.3.refs_1_), channel_id=1, source_target_pairs={{0,0},{16,496},{32,480},{48,464},{64,448},{80,432},{96,416},{112,4... | collective-permute-start | bytes 98312 | tf_op jit(solution)/shard_map/ppermute | solution.py:186
  98.7 2.6 %parts_y.1 = bf16[2,256,768]{2,1,0:T(8,128)(2,1)} custom-call(bf16[2,256,768]{2,1,0:T(8,128)(2,1)S(1)} %get-tuple-element.22.refs_0_, f32[16,4,128]{2,1,0:T(4,128)S(1)} %all-to-all-done.3.refs_1_, f32[32,128]{1,0:T(8,128)S(1)} %collective-permute-done.1.refs_2_.pack_ref.rest_ref), custom_call_target="tpu_custom_call" | custom-call | flops 400000000 | bytes 1000000 | tf_op jit(solution)/shard_map/parts_y/pallas_call | solution.py:26
  101.2 0.0 collective-permute-done.8.refs_0_.refs_2_
  101.2 0.0 collective-permute-done.7.x_ref.refs_0_
  101.2 1.1 %mirror_third.1.x_ref = bf16[256,768]{1,0:T(8,128)(2,1)S(1)} custom-call(bf16[256,768]{1,0:T(8,128)(2,1)S(1)} %collective-permute-done.7.x_ref.refs_0_, f32[32,128]{1,0:T(8,128)S(1)} %collective-permute-done.8.refs_0_.refs_2_), custom_call_target="tpu_custom_call" | custom-call | flops 200000000 | bytes 1000000 | tf_op jit(solution)/shard_map/mirror_third/pallas_call | solution.py:26
  102.4 1.2 %collective-permute-done.9.refs_1_ = f32[16,4,128]{2,1,0:T(4,128)S(1)} collective-permute-done((f32[16,4,128]{2,1,0:T(4,128)S(1)}, f32[16,4,128]{2,1,0:T(4,128)S(1)}, u32[]{:S(2)}, u32[]{:S(2)}) %collective-permute-start.9) | collective-permute-done | bytes 32800 | tf_op jit(solution)/shard_map/ppermute | solution.py:186
  103.5 1.9 %mirror_fourth.1 = bf16[256,768]{1,0:T(8,128)(2,1)} custom-call(bf16[256,768]{1,0:T(8,128)(2,1)S(1)} %mirror_third.1.x_ref, bf16[256,768]{1,0:T(8,128)(2,1)S(1)} %collective-permute-done.7.x_ref.refs_0_, f32[16,4,128]{2,1,0:T(4,128)S(1)} %collective-permute-done.9.refs_1_, f32[32,128]{1,0:T(8,128)S(1)} %collective-permute-done.8.refs_0_.refs_2_), custom_call_target="tpu_custom_call" | custom-call | flops 200000000 | bytes 1000000 | tf_op jit(solution)/shard_map/mirror_fourth/pallas_call | solution.py:26
  (6 shorter events, 0.1 us)
Async XLA Ops:
  0.6 1.4 %copy-start = (bf16[1,2,256,768]{3,2,1,0:T(8,128)(2,1)S(1)}, bf16[1,2,256,768]{3,2,1,0:T(8,128)(2,1)}, u32[]{:S(2)}) copy-start(bf16[1,2,256,768]{3,2,1,0:T(8,128)(2,1)} %param.5) | copy-start | bytes 2359300
  2.8 22.9 %collective-permute-start.2 = (bf16[256,768]{1,0:T(8,128)(2,1)S(1)}, bf16[256,768]{1,0:T(8,128)(2,1)S(1)}, u32[]{:S(2)}, u32[]{:S(2)}) collective-permute-start(bf16[256,768]{1,0:T(8,128)(2,1)S(1)} %get-tuple-element.18), channel_id=1, source_target_pairs={{0,40},{1,41},{2,42},{3,43},{4,44},{5,45},{6,46},{7,47},{16,56},{1... | collective-permute-start | bytes 1179656 | tf_op jit(solution)/shard_map/ppermute | solution.py:242
  7.5 12.2 %copy-start.1 = (f32[1,2,768]{2,1,0:T(2,128)S(1)}, f32[1,2,768]{2,1,0:T(2,128)}, u32[]{:S(2)}) copy-start(f32[1,2,768]{2,1,0:T(2,128)} %param.6) | copy-start | bytes 18436
  7.5 15.8 %all-to-all-start = ((f32[16,4,128]{2,1,0:T(4,128)}), f32[16,4,128]{2,1,0:T(4,128)S(1)}, u32[]{:S(2)}, u32[]{:S(2)}) async-start(f32[16,4,128]{2,1,0:T(4,128)} %first_sums.1), calls=%async_computation | async-start | bytes 65536 | tf_op jit(solution)/shard_map/all_to_all | solution.py:181
  14.7 34.1 %collective-permute-start = (bf16[256,768]{1,0:T(8,128)(2,1)S(1)}, bf16[256,768]{1,0:T(8,128)(2,1)S(1)}, u32[]{:S(2)}, u32[]{:S(2)}) collective-permute-start(bf16[256,768]{1,0:T(8,128)(2,1)S(1)} %get-tuple-element.15), channel_id=1, source_target_pairs={{0,32},{16,48},{32,64},{48,80},{64,96},{80,112},{96,128},{112,144}... | collective-permute-start | bytes 1179656 | tf_op jit(solution)/shard_map/ppermute | solution.py:186
  19.7 0.7 copy-start.2
  25.8 23.1 %collective-permute-start.3 = (bf16[256,768]{1,0:T(8,128)(2,1)S(1)}, bf16[256,768]{1,0:T(8,128)(2,1)S(1)}, u32[]{:S(2)}, u32[]{:S(2)}) collective-permute-start(bf16[256,768]{1,0:T(8,128)(2,1)S(1)} %collective-permute-done.2), channel_id=1, source_target_pairs={{40,32},{41,33},{42,34},{43,35},{44,36},{45,37},{46,38},{47,39},{5... | collective-permute-start | bytes 1179656 | tf_op jit(solution)/shard_map/ppermute | solution.py:247
  29.7 15.3 %all-to-all-start.1 = ((f32[16,4,128]{2,1,0:T(4,128)}), f32[16,4,128]{2,1,0:T(4,128)S(1)}, u32[]{:S(2)}, u32[]{:S(2)}) async-start(f32[16,4,128]{2,1,0:T(4,128)} %parts_sums.1), calls=%async_computation.1 | async-start | bytes 65536 | tf_op jit(solution)/shard_map/all_to_all | solution.py:181
  36.5 12.3 %collective-permute-start.1 = (f32[32,128]{1,0:T(8,128)S(1)}, f32[32,128]{1,0:T(8,128)S(1)}, u32[]{:S(2)}, u32[]{:S(2)}) collective-permute-start(f32[32,128]{1,0:T(8,128)S(1)} %own_pack.1), channel_id=1, source_target_pairs={{0,16},{16,32},{32,48},{48,64},{64,80},{80,96},{96,112},{112,128},... | collective-permute-start | bytes 49160 | tf_op jit(solution)/shard_map/ppermute | solution.py:186
  38.4 10.4 %collective-permute-start.4 = (f32[32,128]{1,0:T(8,128)S(1)}, f32[32,128]{1,0:T(8,128)S(1)}, u32[]{:S(2)}, u32[]{:S(2)}) collective-permute-start(f32[32,128]{1,0:T(8,128)S(1)} %own_pack.1), channel_id=1, source_target_pairs={{0,32},{16,48},{32,64},{48,80},{64,96},{80,112},{96,128},{112,144}... | collective-permute-start | bytes 49160 | tf_op jit(solution)/shard_map/ppermute | solution.py:186
  44.9 8.2 %collective-permute-start.5 = (f32[16,4,128]{2,1,0:T(4,128)S(1)}, f32[16,4,128]{2,1,0:T(4,128)S(1)}, u32[]{:S(2)}, u32[]{:S(2)}) collective-permute-start(f32[16,4,128]{2,1,0:T(4,128)S(1)} %all-to-all-done.1), channel_id=1, source_target_pairs={{0,32},{16,48},{32,64},{48,80},{64,96},{80,112},{96,128},{112,144}... | collective-permute-start | bytes 98312 | tf_op jit(solution)/shard_map/ppermute | solution.py:186
  55.1 19.3 %collective-permute-start.6 = (bf16[256,768]{1,0:T(8,128)(2,1)S(1)}, bf16[256,768]{1,0:T(8,128)(2,1)S(1)}, u32[]{:S(2)}, u32[]{:S(2)}) collective-permute-start(bf16[256,768]{1,0:T(8,128)(2,1)S(1)} %get-tuple-element.25), channel_id=1, source_target_pairs={{0,496},{16,0},{32,16},{48,32},{64,48},{80,64},{96,80},{112,96},{1... | collective-permute-start | bytes 1179656 | tf_op jit(solution)/shard_map/ppermute | solution.py:186
  74.5 26.7 %collective-permute-start.7 = (bf16[256,768]{1,0:T(8,128)(2,1)S(1)}, bf16[256,768]{1,0:T(8,128)(2,1)S(1)}, u32[]{:S(2)}, u32[]{:S(2)}) collective-permute-start(bf16[256,768]{1,0:T(8,128)(2,1)S(1)} %choose.1), channel_id=1, source_target_pairs={{0,0},{16,496},{32,480},{48,464},{64,448},{80,432},{96,416},{112,4... | collective-permute-start | bytes 1179656 | tf_op jit(solution)/shard_map/ppermute | solution.py:186
  81.9 12.0 %all-to-all-start.3 = ((f32[16,4,128]{2,1,0:T(4,128)}), f32[16,4,128]{2,1,0:T(4,128)S(1)}, u32[]{:S(2)}, u32[]{:S(2)}) async-start(f32[16,4,128]{2,1,0:T(4,128)} %get-tuple-element.23), calls=%async_computation.3 | async-start | bytes 65536 | tf_op jit(solution)/shard_map/all_to_all | solution.py:181
  85.4 15.9 %collective-permute-start.8 = (f32[32,128]{1,0:T(8,128)S(1)}, f32[32,128]{1,0:T(8,128)S(1)}, u32[]{:S(2)}, u32[]{:S(2)}) collective-permute-start(f32[32,128]{1,0:T(8,128)S(1)} %late_pack.1), channel_id=1, source_target_pairs={{0,0},{16,496},{32,480},{48,464},{64,448},{80,432},{96,416},{112,4... | collective-permute-start | bytes 49160 | tf_op jit(solution)/shard_map/ppermute | solution.py:186
  93.8 9.7 %collective-permute-start.9 = (f32[16,4,128]{2,1,0:T(4,128)S(1)}, f32[16,4,128]{2,1,0:T(4,128)S(1)}, u32[]{:S(2)}, u32[]{:S(2)}) collective-permute-start(f32[16,4,128]{2,1,0:T(4,128)S(1)} %all-to-all-done.3.refs_1_), channel_id=1, source_target_pairs={{0,0},{16,496},{32,480},{48,464},{64,448},{80,432},{96,416},{112,4... | collective-permute-start | bytes 98312 | tf_op jit(solution)/shard_map/ppermute | solution.py:186
where the time goes:
time: 106 us; the launch traced here: 105 us
  starting transfers between devices  55.7 us (53%)
  blocking collectives  16.4 us (15%)
  Pallas kernels  15.1 us (14%)
  waiting for transfers between devices  13.8 us (13%)
  local copies, waits for them, and re-layouts  2.25 us (2%)
  between operations  2.13 us (2%)
    ppermute x8, starting transfers between devices, send(): lax.ppermute(value, 'section', [(s, target(s) % count) for s in range(cou...  29.6 us
    all_to_all x3, starting transfers between devices, exchange(): return lax.all_to_all(parts, 'tensor', 0, 0, tiled=True)  17.5 us
    all_to_all x1, blocking collectives, exchange(): return lax.all_to_all(parts, 'tensor', 0, 0, tiled=True)  16.4 us
    pallas_call x11, Pallas kernels, run(): pl.pallas_call(kernel, out_shape=out_shape, in_specs=[VMEM] * len(operand...  15.1 us
    all_to_all x3, waiting for transfers between devices, exchange(): return lax.all_to_all(parts, 'tensor', 0, 0, tiled=True)  9.99 us
    ppermute x1, starting transfers between devices, shards(): second_half = lax.ppermute(after(x[1], found), axes, around_x(0))  4.65 us
    ppermute x1, starting transfers between devices, shards(): second_ahead = lax.ppermute(after(second_half, found), axes, around_x(1))  3.9 us
    ppermute x8, waiting for transfers between devices, send(): lax.ppermute(value, 'section', [(s, target(s) % count) for s in range(cou...  3.82 us
  transfers between devices with their start and end apart: 13, of which 5 were waited for; matrix products, arithmetic and copies ran while one was open for 0% of the time, Pallas kernels for 10%

commit v1 on v0

v1 whole, which is shorter than its diff:
```python
import functools

import jax
import jax.numpy as jnp
from jax import lax
from jax.experimental import pallas as pl
from jax.experimental.pallas import tpu as pltpu
from jax.sharding import PartitionSpec as P

D = 12288
HEAD = 128
LAYERS = 2
BLOCK = 128
EPS = 1e-5
SCORE = 1.4426950408889634 / HEAD**0.5

VMEM = pl.BlockSpec(memory_space=pltpu.VMEM)
PARAMS = pltpu.CompilerParams(vmem_limit_bytes=32 * 1024 * 1024)


def call(kernel, out_shape, name, mflop=1, scratch=()):
    several = isinstance(out_shape, tuple)

    def run(*operands):
        return pl.pallas_call(
            kernel,
            out_shape=out_shape,
            in_specs=[VMEM] * len(operands),
            out_specs=(VMEM,) * len(out_shape) if several else VMEM,
            scratch_shapes=[pltpu.VMEM(like.shape, like.dtype) for like in scratch],
            compiler_params=PARAMS,
            cost_estimate=pl.CostEstimate(
                flops=mflop * 1_000_000, bytes_accessed=1_000_000, transcendentals=mflop * 2_000
            ),
            name=name,
        )(*operands)

    return run


def f32(*shape):
    return jax.ShapeDtypeStruct(shape, jnp.float32)


def bf16(*shape):
    return jax.ShapeDtypeStruct(shape, jnp.bfloat16)


def column(total):
    inv = lax.rsqrt(total / D + EPS)
    rows = [jnp.broadcast_to(inv[i : i + 1], (BLOCK, BLOCK)).T for i in range(inv.shape[0])]
    return jnp.concatenate(rows, axis=0)


def head_layer(xf, scale, ngain, kgain):
    length = xf.shape[0]
    keep = lax.broadcasted_iota(jnp.int32, (BLOCK, BLOCK), 1) <= lax.broadcasted_iota(jnp.int32, (BLOCK, BLOCK), 0)
    h = xf * scale * ngain
    query = h.astype(jnp.bfloat16)
    keys = (h * (kgain * SCORE)).astype(jnp.bfloat16)
    values = jnp.concatenate([query, jnp.ones((length, HEAD), jnp.bfloat16)], axis=1)
    out = []
    for i in range(length // BLOCK):
        here = slice(i * BLOCK, (i + 1) * BLOCK)
        seen = (i + 1) * BLOCK
        s = lax.dot_general(
            query[here], keys[:seen], (((1,), (1,)), ((), ())), preferred_element_type=jnp.float32
        )
        last = jnp.where(keep, s[:, i * BLOCK :], jnp.float32(-1e30))
        s = last if i == 0 else jnp.concatenate([s[:, : i * BLOCK], last], axis=1)
        p = jnp.exp2(s - jnp.max(s, axis=1, keepdims=True)).astype(jnp.bfloat16)
        o = jnp.dot(p, values[:seen], preferred_element_type=jnp.float32)
        out.append((xf[here] + o[:, :HEAD] / o[:, HEAD:]).astype(jnp.bfloat16))
    return jnp.concatenate(out, axis=0)


def token_rows(squares):
    rows = []
    for sq in squares:
        for i in range(sq.shape[0] // BLOCK):
            rows.append(jnp.sum(sq[i * BLOCK : (i + 1) * BLOCK].T, axis=0, keepdims=True))
    return jnp.concatenate(rows, axis=0)


def token_sums(squares, out_ref):
    out_ref[...] = jnp.broadcast_to(token_rows(squares)[None], out_ref.shape)


def lanes(head):
    return slice(head * HEAD, (head + 1) * HEAD)


class Pack:
    def __init__(self, heads, batch, blocks):
        self.heads, self.rows = heads, batch * blocks
        self.slot = 2 * LAYERS * heads
        self.step = self.slot + 1
        self.size = -(-(self.step + 1) // 8) * 8
        self.full = 2 * self.size + 2 * LAYERS * self.rows

    def gains(self, ref, layer, head):
        base = layer // LAYERS * self.size
        at = [base + (part * LAYERS + layer % LAYERS) * self.heads + head for part in range(2)]
        return [ref[i : i + 1, :] for i in at]

    def sums(self, layer):
        return slice(2 * self.size + layer * self.rows, 2 * self.size + (layer + 1) * self.rows)

    def second(self, ref, section=0):
        at = section * self.size + self.slot
        return ref[at : at + 1, :] > 0.5

    def late(self, ref, section=0):
        at = section * self.size + self.step
        return ref[at : at + 1, :] > 0.5


def first_kernel(x_ref, copy_ref, out_ref):
    batch, _, width = x_ref.shape
    found = []
    for b in range(batch):
        sq = 0.0
        for head in range(width // HEAD):
            xb = x_ref[b, :, lanes(head)]
            copy_ref[b, :, lanes(head)] = xb
            xf = xb.astype(jnp.float32)
            sq = sq + xf * xf
        found.append(sq)
    token_sums(found, out_ref)


def one_layer(pack, layer, x_refs, totals, pack_ref, y_ref):
    blocks = x_refs[0].shape[0] // BLOCK
    found = []
    for b, x_ref in enumerate(x_refs):
        scale = column(totals[b * blocks : (b + 1) * blocks])
        sq = 0.0
        for head in range(pack.heads):
            xf = x_ref[:, lanes(head)].astype(jnp.float32)
            y = head_layer(xf, scale, *pack.gains(pack_ref, layer, head))
            if y_ref is not None:
                y_ref[b, :, lanes(head)] = y
            yf = y.astype(jnp.float32)
            sq = sq + yf * yf
        found.append(sq)
    return found


def added(parts_ref):
    return jnp.sum(parts_ref[...], axis=0)


def halves(ref):
    return [ref.at[b] for b in range(ref.shape[0])]


def either(condition, there, here):
    return jnp.where(condition, there.astype(jnp.float32), here.astype(jnp.float32)).astype(jnp.bfloat16)


def layer1_kernel(pack, x_ref, parts_ref, own_ref, y_ref, out_ref):
    token_sums(one_layer(pack, 0, halves(x_ref), added(parts_ref), own_ref, y_ref), out_ref)


def layer2_kernel(pack, x_ref, parts_ref, own_ref, next_ref, y_ref, pick_ref, out_ref):
    token_sums(one_layer(pack, 1, halves(x_ref), added(parts_ref), own_ref, y_ref), out_ref)
    second = pack.second(next_ref)
    for head in range(pack.heads):
        pick_ref[:, lanes(head)] = either(second, y_ref[1, :, lanes(head)], y_ref[0, :, lanes(head)])


def choose_kernel(pack, y_ref, carry_ref, pack_ref, out_ref):
    second, late = pack.second(pack_ref), pack.late(pack_ref)
    for head in range(pack.heads):
        at = lanes(head)
        out_ref[:, at] = either(late, carry_ref[:, at], either(second, y_ref[1, :, at], y_ref[0, :, at]))


def layer3_kernel(pack, x_ref, own_ref, next_ref, *refs):
    *parts_refs, out_ref = refs
    out_ref[: pack.size, :] = own_ref[...]
    out_ref[pack.size : 2 * pack.size, :] = next_ref[...]
    for layer, parts_ref in enumerate(parts_refs):
        out_ref[pack.sums(layer), :] = added(parts_ref)
    last = len(parts_refs)
    found = one_layer(pack, 0, halves(x_ref), out_ref[pack.sums(last - 1), :], next_ref, None)
    out_ref[pack.sums(last), :] = token_rows(found)


def parts_kernel(pack, pack_ref, out_ref):
    out_ref[...] = jnp.broadcast_to(pack_ref[pack.sums(2 * LAYERS - 1), :][None], out_ref.shape)


def late_kernel(pack, pack_ref, parts_ref, out_ref):
    out_ref[...] = pack_ref[...]
    out_ref[pack.sums(2 * LAYERS - 1), :] = added(parts_ref)


def repeat_kernel(pack, x_ref, pack_ref, out_ref, y_ref):
    refs = [x_ref, out_ref, y_ref, out_ref]
    for layer in range(2 * LAYERS - 1):
        one_layer(pack, layer, halves(refs[layer]), pack_ref[pack.sums(layer), :], pack_ref, refs[layer + 1])


def layer4_kernel(pack, x_ref, parts_ref, pack_ref, y_ref):
    one_layer(pack, 2 * LAYERS - 1, halves(x_ref), added(parts_ref), pack_ref, y_ref)


def mirror_kernel(pack, x_ref, pack_ref, out_ref, y_ref):
    blocks = x_ref.shape[0] // BLOCK
    second, late = pack.second(pack_ref, 1), pack.late(pack_ref, 1)
    refs = [x_ref, y_ref, out_ref]
    for at in range(LAYERS):
        layer = LAYERS + at
        totals = pack_ref[pack.sums(layer), :]
        scale = column(jnp.where(second, totals[blocks : 2 * blocks], totals[:blocks]))
        for head in range(pack.heads):
            xf = refs[at][:, lanes(head)].astype(jnp.float32)
            y = head_layer(xf, scale, *pack.gains(pack_ref, layer, head))
            if at == LAYERS - 1:
                y = either(late, y, x_ref[:, lanes(head)])
            refs[at + 1][:, lanes(head)] = y


def exchange(parts):
    return lax.all_to_all(parts, "tensor", 0, 0, tiled=True)


def send(value, target):
    count = lax.axis_size("section")
    return lax.ppermute(value, "section", [(s, target(s) % count) for s in range(count)])


def after(value, *earlier):
    return lax.optimization_barrier((value, *earlier))[0]


def shards(held, norm_gain, key_gain, evict_slot, evict_step):
    x = held[0]
    batch, length, width = x.shape
    heads = width // HEAD
    pack = Pack(heads, batch, length // BLOCK)
    sections, members = lax.axis_size("section"), lax.axis_size("tensor")
    both, one = bf16(*x.shape), bf16(length, width)
    sums, full = f32(members, pack.rows, BLOCK), f32(pack.full, HEAD)

    def run(kernel, out, *operands, mflop=400, scratch=()):
        return call(functools.partial(kernel, pack), out, kernel.__name__, mflop, scratch)(*operands)

    facts = jnp.concatenate([evict_slot, evict_step]).astype(jnp.float32)
    own = jnp.concatenate(
        [
            norm_gain.reshape(-1, HEAD),
            key_gain.reshape(-1, HEAD),
            jnp.broadcast_to(facts[:, None], (2, HEAD)),
            jnp.zeros((pack.size - pack.step - 1, HEAD), jnp.float32),
        ],
        axis=0,
    )

    ahead = send(own, lambda s: s - 1)
    x, found = call(first_kernel, (both, sums), "first_kernel")(x)
    moved = send(after(x, ahead), lambda s: s + 2)
    parts1 = exchange(found)
    y, found = run(layer1_kernel, (both, sums), after(x, ahead), parts1, own)
    parts2 = exchange(found)
    y, pick, found = run(layer2_kernel, (both, one, sums), y, parts2, own, ahead)
    carry = send(after(pick, found), lambda s: s + 1)
    parts3 = exchange(found)
    found = run(layer3_kernel, full, y, own, ahead, parts1, parts2, parts3)
    behind = send(found, lambda s: s + 2)
    kept = run(choose_kernel, one, y, after(carry, behind), own, mflop=1)
    kept = send(kept, lambda s: sections - 1 - s)

    parts4 = exchange(run(parts_kernel, sums, behind, mflop=1))
    y = run(repeat_kernel, both, moved, behind, mflop=1200, scratch=[both])
    parts4 = after(parts4, y)
    late = send(run(late_kernel, full, behind, parts4, mflop=1), lambda s: -s)
    final = run(layer4_kernel, both, y, parts4, behind)

    stored = run(mirror_kernel, one, kept, late, mflop=400, scratch=[one])
    return (final[None], stored[None])


def solution(mesh):
    return jax.shard_map(
        shards,
        mesh=mesh,
        in_specs=(
            P("section", None, None, "tensor"),
            P("section", None, "tensor"),
            P("section", None, "tensor"),
            P("section"),
            P("section"),
        ),
        out_specs=(P("section", None, None, "tensor"), P("section", None, "tensor")),
        check_vma=False,
    )
```

time: 106 us -> 106 us (level)
  the two profiles are of different devices: /device:TPU:128 before, /device:TPU:69 now
where the time goes in v1:
time: 106 us; the launch traced here: 105 us
  starting transfers between devices  38.9 us (37%)
  blocking collectives  29.6 us (28%)
  waiting for transfers between devices  16.6 us (16%)
  Pallas kernels  16.2 us (15%)
  between operations  2.07 us (2%)
  local copies, waits for them, and re-layouts  1.99 us (2%)
    all_to_all x2, blocking collectives, exchange(): return lax.all_to_all(parts, 'tensor', 0, 0, tiled=True)  29.6 us
    ppermute x6, starting transfers between devices, send(): lax.ppermute(value, 'section', [(s, target(s) % count) for s in range(cou...  27.9 us
    pallas_call x10, Pallas kernels, run(): pl.pallas_call(kernel, out_shape=out_shape, in_specs=[VMEM] * len(operand...  16.2 us
    ppermute x6, waiting for transfers between devices, send(): lax.ppermute(value, 'section', [(s, target(s) % count) for s in range(cou...  13.1 us
    all_to_all x2, starting transfers between devices, exchange(): return lax.all_to_all(parts, 'tensor', 0, 0, tiled=True)  11.1 us
    all_to_all x2, waiting for transfers between devices, exchange(): return lax.all_to_all(parts, 'tensor', 0, 0, tiled=True)  3.48 us
  transfers between devices with their start and end apart: 8, of which 4 were waited for; matrix products, arithmetic and copies ran while one was open for 0% of the time, Pallas kernels for 12%

profile of v1, /device:TPU:69, one launch (start us, length us, event | category | flops | bytes accessed | tf_op | source)
XLA Modules:
  0.0 105.5 jit_solution(15818271206407535408)
XLA Ops:
  0.6 0.0 copy-start
  0.6 1.1 %copy-done = bf16[1,2,256,768]{3,2,1,0:T(8,128)(2,1)S(1)} copy-done((bf16[1,2,256,768]{3,2,1,0:T(8,128)(2,1)S(1)}, bf16[1,2,256,768]{3,2,1,0:T(8,128)(2,1)}, u32[]{:S(2)}) %copy-start) | copy-done | bytes 786456
  1.8 0.9 first_kernel.1
  2.7 7.6 %all-to-all-start = ((f32[16,4,128]{2,1,0:T(4,128)}), f32[16,4,128]{2,1,0:T(4,128)S(1)}, u32[]{:S(2)}, u32[]{:S(2)}) async-start(f32[16,4,128]{2,1,0:T(4,128)} %get-tuple-element.15), calls=%async_computation | async-start | bytes 65536 | tf_op jit(solution)/shard_map/all_to_all | solution.py:226
  10.3 0.0 copy-start.1
  11.6 0.1 add_convert_fusion
  11.7 0.1 pad.2.clone
  11.7 0.1 pad.3.clone
  11.8 0.0 copy-done.1
  11.8 0.0 copy-start.2
  11.8 0.7 copy-done.2
  12.5 0.1 maximum_maximum_fusion.own_ref.pack_ref
  12.6 2.9 %collective-permute-start = (f32[32,128]{1,0:T(8,128)S(1)}, f32[32,128]{1,0:T(8,128)S(1)}, u32[]{:S(2)}, u32[]{:S(2)}) collective-permute-start(f32[32,128]{1,0:T(8,128)S(1)} %maximum_maximum_fusion.own_ref.pack_ref), channel_id=1, source_target_pairs={{0,496},{16,0},{32,16},{48,32},{64,48},{80,64},{96,80},{112,96},{1... | collective-permute-start | bytes 49160 | tf_op jit(solution)/shard_map/ppermute | solution.py:231
  15.5 4.6 %collective-permute-done.next_ref = f32[32,128]{1,0:T(8,128)S(1)} collective-permute-done((f32[32,128]{1,0:T(8,128)S(1)}, f32[32,128]{1,0:T(8,128)S(1)}, u32[]{:S(2)}, u32[]{:S(2)}) %collective-permute-start) | collective-permute-done | bytes 16416 | tf_op jit(solution)/shard_map/ppermute | solution.py:231
  20.0 3.5 %collective-permute-start.1 = (bf16[2,256,768]{2,1,0:T(8,128)(2,1)S(1)}, bf16[2,256,768]{2,1,0:T(8,128)(2,1)S(1)}, u32[]{:S(2)}, u32[]{:S(2)}) collective-permute-start(bf16[2,256,768]{2,1,0:T(8,128)(2,1)S(1)} %get-tuple-element.14.x_ref), channel_id=1, source_target_pairs={{0,32},{16,48},{32,64},{48,80},{64,96},{80,112},{96,128},{112,144}... | collective-permute-start | bytes 2359304 | tf_op jit(solution)/shard_map/ppermute | solution.py:231
  23.6 0.0 all-to-all-done.parts_ref.refs_0_
  23.6 1.8 %layer1_kernel.1 = (bf16[2,256,768]{2,1,0:T(8,128)(2,1)S(1)}, f32[16,4,128]{2,1,0:T(4,128)S(1)}) custom-call(bf16[2,256,768]{2,1,0:T(8,128)(2,1)S(1)} %get-tuple-element.14.x_ref, f32[16,4,128]{2,1,0:T(4,128)S(1)} %all-to-all-done.parts_ref.refs_0_, f32[32,128]{1,0:T(8,128)S(1)} %maximum_maximum_fusion.own_ref.pack_ref), custom_call_target="tpu_custom_call" | custom-call | flops 400000000 | bytes 1000000 | tf_op jit(solution)/shard_map/layer1_kernel/pallas_call | solution.py:25
  25.4 15.3 %all_to_all.20.parts_ref.refs_1_ = f32[16,4,128]{2,1,0:T(4,128)S(1)} all-to-all(f32[16,4,128]{2,1,0:T(4,128)S(1)} %get-tuple-element.17), channel_id=1, replica_groups=mesh['section'=32,'tensor'=16] {'tensor'}, dimensions={0} | all-to-all | bytes 65536 | tf_op jit(solution)/shard_map/all_to_all | solution.py:226
  40.6 2.0 %layer2_kernel.1 = (bf16[2,256,768]{2,1,0:T(8,128)(2,1)S(1)}, bf16[256,768]{1,0:T(8,128)(2,1)S(1)}, f32[16,4,128]{2,1,0:T(4,128)S(1)}) custom-call(bf16[2,256,768]{2,1,0:T(8,128)(2,1)S(1)} %get-tuple-element.16.x_ref, f32[16,4,128]{2,1,0:T(4,128)S(1)} %all_to_all.20.parts_ref.refs_1_, f32[32,128]{1,0:T(8,128)S(1)} %maximum_maximum_fusion.own_ref.pack_ref, ...), custom_call_target="tpu_custom_call" | custom-call | flops 400000000 | bytes 1000000 | tf_op jit(solution)/shard_map/layer2_kernel/pallas_call | solution.py:25
  42.6 3.1 %collective-permute-start.3 = (bf16[256,768]{1,0:T(8,128)(2,1)S(1)}, bf16[256,768]{1,0:T(8,128)(2,1)S(1)}, u32[]{:S(2)}, u32[]{:S(2)}) collective-permute-start(bf16[256,768]{1,0:T(8,128)(2,1)S(1)} %get-tuple-element.22), channel_id=1, source_target_pairs={{0,16},{16,32},{32,48},{48,64},{64,80},{80,96},{96,112},{112,128},... | collective-permute-start | bytes 1179656 | tf_op jit(solution)/shard_map/ppermute | solution.py:231
  45.7 14.3 %all_to_all.21.refs_2_ = f32[16,4,128]{2,1,0:T(4,128)S(1)} all-to-all(f32[16,4,128]{2,1,0:T(4,128)S(1)} %get-tuple-element.19), channel_id=1, replica_groups=mesh['section'=32,'tensor'=16] {'tensor'}, dimensions={0} | all-to-all | bytes 65536 | tf_op jit(solution)/shard_map/all_to_all | solution.py:226
  60.0 1.8 %layer3_kernel.1 = f32[80,128]{1,0:T(8,128)S(1)} custom-call(bf16[2,256,768]{2,1,0:T(8,128)(2,1)S(1)} %get-tuple-element.18.x_ref.y_ref, f32[32,128]{1,0:T(8,128)S(1)} %maximum_maximum_fusion.own_ref.pack_ref, f32[32,128]{1,0:T(8,128)S(1)} %collective-permute-done.next_ref, f32[16,4,128]{2,1,0:T(4,128)S(1)} %all-to-all-done.parts_ref.refs_0_, ...), custom_call_target="tpu_custom_call" | custom-call | flops 400000000 | bytes 1000000 | tf_op jit(solution)/shard_map/layer3_kernel/pallas_call | solution.py:25
  61.8 3.2 %collective-permute-start.2 = (f32[80,128]{1,0:T(8,128)S(1)}, f32[80,128]{1,0:T(8,128)S(1)}, u32[]{:S(2)}, u32[]{:S(2)}) collective-permute-start(f32[80,128]{1,0:T(8,128)S(1)} %layer3_kernel.1), channel_id=1, source_target_pairs={{0,32},{16,48},{32,64},{48,80},{64,96},{80,112},{96,128},{112,144}... | collective-permute-start | bytes 122888 | tf_op jit(solution)/shard_map/ppermute | solution.py:231
  65.1 3.0 %collective-permute-done.2.pack_ref = f32[80,128]{1,0:T(8,128)S(1)} collective-permute-done((f32[80,128]{1,0:T(8,128)S(1)}, f32[80,128]{1,0:T(8,128)S(1)}, u32[]{:S(2)}, u32[]{:S(2)}) %collective-permute-start.2) | collective-permute-done | bytes 40992 | tf_op jit(solution)/shard_map/ppermute | solution.py:231
  68.1 0.0 collective-permute-done.3.carry_ref
  68.1 0.2 choose_kernel.1
  68.2 13.1 %collective-permute-start.4 = (bf16[256,768]{1,0:T(8,128)(2,1)S(1)}, bf16[256,768]{1,0:T(8,128)(2,1)S(1)}, u32[]{:S(2)}, u32[]{:S(2)}) collective-permute-start(bf16[256,768]{1,0:T(8,128)(2,1)S(1)} %choose_kernel.1), channel_id=1, source_target_pairs={{0,496},{16,480},{32,464},{48,448},{64,432},{80,416},{96,400},{112... | collective-permute-start | bytes 1179656 | tf_op jit(solution)/shard_map/ppermute | solution.py:231
  81.4 0.6 parts_kernel.1
  82.0 3.5 %all-to-all-start.3 = ((f32[16,4,128]{2,1,0:T(4,128)}), f32[16,4,128]{2,1,0:T(4,128)S(1)}, u32[]{:S(2)}, u32[]{:S(2)}) async-start(f32[16,4,128]{2,1,0:T(4,128)} %parts_kernel.1), calls=%async_computation.3 | async-start | bytes 65536 | tf_op jit(solution)/shard_map/all_to_all | solution.py:226
  85.5 0.0 collective-permute-done.1.x_ref
  85.5 3.8 %repeat_kernel.1.x_ref = bf16[2,256,768]{2,1,0:T(8,128)(2,1)S(1)} custom-call(bf16[2,256,768]{2,1,0:T(8,128)(2,1)S(1)} %collective-permute-done.1.x_ref, f32[80,128]{1,0:T(8,128)S(1)} %collective-permute-done.2.pack_ref), custom_call_target="tpu_custom_call" | custom-call | flops 1200000000 | bytes 1000000 | tf_op jit(solution)/shard_map/repeat_kernel/pallas_call | solution.py:25
  89.3 3.5 %all-to-all-done.3.parts_ref = f32[16,4,128]{2,1,0:T(4,128)S(1)} async-done(((f32[16,4,128]{2,1,0:T(4,128)}), f32[16,4,128]{2,1,0:T(4,128)S(1)}, u32[]{:S(2)}, u32[]{:S(2)}) %all-to-all-start.3) | async-done | bytes 32800 | tf_op jit(solution)/shard_map/all_to_all | solution.py:226
  92.8 2.1 %collective-permute-start.5 = (f32[80,128]{1,0:T(8,128)S(1)}, f32[80,128]{1,0:T(8,128)S(1)}, u32[]{:S(2)}, u32[]{:S(2)}) collective-permute-start(f32[80,128]{1,0:T(8,128)S(1)} %late_kernel.1), channel_id=1, source_target_pairs={{0,0},{16,496},{32,480},{48,464},{64,448},{80,432},{96,416},{112,4... | collective-permute-start | bytes 122888 | tf_op jit(solution)/shard_map/ppermute | solution.py:231
  94.9 2.6 %layer4_kernel.1 = bf16[2,256,768]{2,1,0:T(8,128)(2,1)} custom-call(bf16[2,256,768]{2,1,0:T(8,128)(2,1)S(1)} %repeat_kernel.1.x_ref, f32[16,4,128]{2,1,0:T(4,128)S(1)} %all-to-all-done.3.parts_ref, f32[80,128]{1,0:T(8,128)S(1)} %collective-permute-done.2.pack_ref), custom_call_target="tpu_custom_call" | custom-call | flops 400000000 | bytes 1000000 | tf_op jit(solution)/shard_map/layer4_kernel/pallas_call | solution.py:25
  97.5 5.5 %collective-permute-done.5.pack_ref = f32[80,128]{1,0:T(8,128)S(1)} collective-permute-done((f32[80,128]{1,0:T(8,128)S(1)}, f32[80,128]{1,0:T(8,128)S(1)}, u32[]{:S(2)}, u32[]{:S(2)}) %collective-permute-start.5) | collective-permute-done | bytes 40992 | tf_op jit(solution)/shard_map/ppermute | solution.py:231
  103.0 0.0 collective-permute-done.4.x_ref
  103.0 2.5 %mirror_kernel.1 = bf16[256,768]{1,0:T(8,128)(2,1)} custom-call(bf16[256,768]{1,0:T(8,128)(2,1)S(1)} %collective-permute-done.4.x_ref, f32[80,128]{1,0:T(8,128)S(1)} %collective-permute-done.5.pack_ref), custom_call_target="tpu_custom_call" | custom-call | flops 400000000 | bytes 1000000 | tf_op jit(solution)/shard_map/mirror_kernel/pallas_call | solution.py:25
  (4 shorter events, 0.0 us)
Async XLA Ops:
  0.6 1.1 %copy-start = (bf16[1,2,256,768]{3,2,1,0:T(8,128)(2,1)S(1)}, bf16[1,2,256,768]{3,2,1,0:T(8,128)(2,1)}, u32[]{:S(2)}) copy-start(bf16[1,2,256,768]{3,2,1,0:T(8,128)(2,1)} %param.5) | copy-start | bytes 2359300
  2.7 20.9 %all-to-all-start = ((f32[16,4,128]{2,1,0:T(4,128)}), f32[16,4,128]{2,1,0:T(4,128)S(1)}, u32[]{:S(2)}, u32[]{:S(2)}) async-start(f32[16,4,128]{2,1,0:T(4,128)} %get-tuple-element.15), calls=%async_computation | async-start | bytes 65536 | tf_op jit(solution)/shard_map/all_to_all | solution.py:226
  10.3 1.6 %copy-start.1 = (f32[1,2,768]{2,1,0:T(2,128)S(1)}, f32[1,2,768]{2,1,0:T(2,128)}, u32[]{:S(2)}) copy-start(f32[1,2,768]{2,1,0:T(2,128)} %param.6) | copy-start | bytes 18436
  11.8 0.7 copy-start.2
  12.6 7.5 %collective-permute-start = (f32[32,128]{1,0:T(8,128)S(1)}, f32[32,128]{1,0:T(8,128)S(1)}, u32[]{:S(2)}, u32[]{:S(2)}) collective-permute-start(f32[32,128]{1,0:T(8,128)S(1)} %maximum_maximum_fusion.own_ref.pack_ref), channel_id=1, source_target_pairs={{0,496},{16,0},{32,16},{48,32},{64,48},{80,64},{96,80},{112,96},{1... | collective-permute-start | bytes 49160 | tf_op jit(solution)/shard_map/ppermute | solution.py:231
  20.0 65.4 %collective-permute-start.1 = (bf16[2,256,768]{2,1,0:T(8,128)(2,1)S(1)}, bf16[2,256,768]{2,1,0:T(8,128)(2,1)S(1)}, u32[]{:S(2)}, u32[]{:S(2)}) collective-permute-start(bf16[2,256,768]{2,1,0:T(8,128)(2,1)S(1)} %get-tuple-element.14.x_ref), channel_id=1, source_target_pairs={{0,32},{16,48},{32,64},{48,80},{64,96},{80,112},{96,128},{112,144}... | collective-permute-start | bytes 2359304 | tf_op jit(solution)/shard_map/ppermute | solution.py:231
  42.6 25.4 %collective-permute-start.3 = (bf16[256,768]{1,0:T(8,128)(2,1)S(1)}, bf16[256,768]{1,0:T(8,128)(2,1)S(1)}, u32[]{:S(2)}, u32[]{:S(2)}) collective-permute-start(bf16[256,768]{1,0:T(8,128)(2,1)S(1)} %get-tuple-element.22), channel_id=1, source_target_pairs={{0,16},{16,32},{32,48},{48,64},{64,80},{80,96},{96,112},{112,128},... | collective-permute-start | bytes 1179656 | tf_op jit(solution)/shard_map/ppermute | solution.py:231
  61.8 6.3 %collective-permute-start.2 = (f32[80,128]{1,0:T(8,128)S(1)}, f32[80,128]{1,0:T(8,128)S(1)}, u32[]{:S(2)}, u32[]{:S(2)}) collective-permute-start(f32[80,128]{1,0:T(8,128)S(1)} %layer3_kernel.1), channel_id=1, source_target_pairs={{0,32},{16,48},{32,64},{48,80},{64,96},{80,112},{96,128},{112,144}... | collective-permute-start | bytes 122888 | tf_op jit(solution)/shard_map/ppermute | solution.py:231
  68.2 34.8 %collective-permute-start.4 = (bf16[256,768]{1,0:T(8,128)(2,1)S(1)}, bf16[256,768]{1,0:T(8,128)(2,1)S(1)}, u32[]{:S(2)}, u32[]{:S(2)}) collective-permute-start(bf16[256,768]{1,0:T(8,128)(2,1)S(1)} %choose_kernel.1), channel_id=1, source_target_pairs={{0,496},{16,480},{32,464},{48,448},{64,432},{80,416},{96,400},{112... | collective-permute-start | bytes 1179656 | tf_op jit(solution)/shard_map/ppermute | solution.py:231
  82.0 10.8 %all-to-all-start.3 = ((f32[16,4,128]{2,1,0:T(4,128)}), f32[16,4,128]{2,1,0:T(4,128)S(1)}, u32[]{:S(2)}, u32[]{:S(2)}) async-start(f32[16,4,128]{2,1,0:T(4,128)} %parts_kernel.1), calls=%async_computation.3 | async-start | bytes 65536 | tf_op jit(solution)/shard_map/all_to_all | solution.py:226
  92.8 10.2 %collective-permute-start.5 = (f32[80,128]{1,0:T(8,128)S(1)}, f32[80,128]{1,0:T(8,128)S(1)}, u32[]{:S(2)}, u32[]{:S(2)}) collective-permute-start(f32[80,128]{1,0:T(8,128)S(1)} %late_kernel.1), channel_id=1, source_target_pairs={{0,0},{16,496},{32,480},{48,464},{64,448},{80,432},{96,416},{112,4... | collective-permute-start | bytes 122888 | tf_op jit(solution)/shard_map/ppermute | solution.py:231
